TPU v7x, 128 devices: a whole 4x4x4 slice. The times are simulated.
128 devices in a mesh: replica: 8 (over x_hi, z), zero: 16 (over x_lo, y, core).
Axes of the slice: x: 4 (x_hi: 2, x_lo: 2; x = x_hi * 2 + x_lo), y: 4, z: 4, core: 2. Of those that a mesh axis runs over, the one named last changes fastest.
Arguments:
- grads_pair: bfloat16 [128, 2, 64, 28672], P(('replica', 'zero')), may hold values from -24 to 24
- grads_down: bfloat16 [128, 128, 8192], P(('replica', 'zero')), may hold values from -24 to 24
- inner_pair: float32 [8, 2, 64, 28672], P('replica', None, None, 'zero'), may hold values from -6 to 6
- inner_down: float32 [8, 128, 8192], P('replica', None, 'zero'), may hold values from -6 to 6
- first_pair: float32 [8, 2, 64, 28672], P('replica', None, None, 'zero'), may hold values from -2.4 to 2.4
- first_down: float32 [8, 128, 8192], P('replica', None, 'zero'), may hold values from -2.4 to 2.4
- second_pair: float32 [8, 2, 64, 28672], P('replica', None, None, 'zero'), may hold values from 0.1 to 2
- second_down: float32 [8, 128, 8192], P('replica', None, 'zero'), may hold values from 0.1 to 2
- anchor_pair: float32 [2, 64, 28672], P(None, None, 'zero'), may hold values from -6 to 6
- anchor_down: float32 [128, 8192], P(None, 'zero'), may hold values from -6 to 6
- velocity_pair: float32 [2, 64, 28672], P(None, None, 'zero'), may hold values from -1.8 to 1.8
- velocity_down: float32 [128, 8192], P(None, 'zero'), may hold values from -1.8 to 1.8
Outputs:
- weights_pair: bfloat16 [2, 64, 28672], replicated
- weights_down: bfloat16 [128, 8192], replicated
- anchor_pair_next: float32 [2, 64, 28672], P(None, 'replica', 'zero')
- anchor_down_next: float32 [128, 8192], P('replica', 'zero')
- velocity_pair_next: float32 [2, 64, 28672], P(None, 'replica', 'zero')
- velocity_down_next: float32 [128, 8192], P('replica', 'zero')
All inputs are finite; a program needn't handle non-finite values.
Results may differ from a plain program's by a relative error of at most 0.00185.
Values may be sent and summed in bfloat16 or wider, within the bound.
A program may use at most 128 MiB of HBM per device.

v0:
```python
import jax
import jax.numpy as jnp
from jax import lax
from jax.sharding import PartitionSpec as P

INNER_STEP = 500


beta_one = 0.9
beta_two = 0.95
inner_rate = 0.2
decay_rate = 0.1
outer_rate = 0.7
momentum_keep = 0.9
epsilon_add = 1e-08


def inner_update(summed, inner, first, second):
    first_new = beta_one * first + (1.0 - beta_one) * summed
    second_new = beta_two * second + (1.0 - beta_two) * summed * summed
    first_fix = 1.0 - beta_one**INNER_STEP
    second_fix = 1.0 - beta_two**INNER_STEP
    ratio = first_new / first_fix / (jnp.sqrt(second_new / second_fix) + epsilon_add)
    return inner - inner_rate * (ratio + decay_rate * inner)


def nesterov(pseudo, anchor, velocity):
    velocity_next = momentum_keep * velocity + pseudo
    anchor_next = anchor - outer_rate * (pseudo + momentum_keep * velocity_next)
    return (anchor_next, velocity_next)


def own_rows(array, position, count, axis_dim):
    return lax.dynamic_slice_in_dim(array, position * count, count, axis_dim)


def body(
    grads_pair,
    grads_down,
    inner_pair,
    inner_down,
    first_pair,
    first_down,
    second_pair,
    second_down,
    anchor_pair,
    anchor_down,
    velocity_pair,
    velocity_down,
):
    pieces_pair, pieces_down = (
        lax.all_to_all(grads_pair, "zero", split_axis=3, concat_axis=0, tiled=True),
        lax.all_to_all(grads_down[:, None], "zero", split_axis=3, concat_axis=0, tiled=True),
    )
    summed_pair = jnp.sum(pieces_pair.astype(jnp.float32), axis=0)
    summed_down = jnp.sum(pieces_down.astype(jnp.float32), axis=0)[0]
    inner_pair_new = inner_update(summed_pair, inner_pair[0], first_pair[0], second_pair[0])
    inner_down_new = inner_update(summed_down, inner_down[0], first_down[0], second_down[0])
    drift_pair = anchor_pair - inner_pair_new
    drift_down = anchor_down - inner_down_new
    replicas = lax.axis_size("replica")
    position = lax.axis_index("replica")
    rows_pair = anchor_pair.shape[1] // replicas
    rows_down = anchor_down.shape[0] // replicas
    total_pair, total_down = lax.psum((drift_pair, drift_down), "replica")
    anchor_pair_new, velocity_pair_new = nesterov(total_pair / replicas, anchor_pair, velocity_pair)
    anchor_down_new, velocity_down_new = nesterov(total_down / replicas, anchor_down, velocity_down)
    weights_pair, weights_down = (
        lax.all_gather(anchor_pair_new.astype(jnp.bfloat16), "zero", axis=2, tiled=True),
        lax.all_gather(anchor_down_new.astype(jnp.bfloat16), "zero", axis=1, tiled=True),
    )
    anchor_pair_out = own_rows(anchor_pair_new, position, rows_pair, 1)
    anchor_down_out = own_rows(anchor_down_new, position, rows_down, 0)
    velocity_pair_out = own_rows(velocity_pair_new, position, rows_pair, 1)
    velocity_down_out = own_rows(velocity_down_new, position, rows_down, 0)
    return (
        weights_pair,
        weights_down,
        anchor_pair_out,
        anchor_down_out,
        velocity_pair_out,
        velocity_down_out,
    )


def solution(mesh):
    in_specs = (
        P(("replica", "zero"), None, None, None),
        P(("replica", "zero"), None, None),
        P("replica", None, None, "zero"),
        P("replica", None, "zero"),
        P("replica", None, None, "zero"),
        P("replica", None, "zero"),
        P("replica", None, None, "zero"),
        P("replica", None, "zero"),
        P(None, None, "zero"),
        P(None, "zero"),
        P(None, None, "zero"),
        P(None, "zero"),
    )
    out_specs = (
        P(),
        P(),
        P(None, "replica", "zero"),
        P("replica", "zero"),
        P(None, "replica", "zero"),
        P("replica", "zero"),
    )
    return jax.shard_map(body, mesh=mesh, in_specs=in_specs, out_specs=out_specs, check_vma=False)
```

profile of v0, /device:TPU:1, one launch (start us, length us, event | category | flops | bytes accessed | tf_op | source)
XLA Modules:
  0.0 466.3 jit_solution(6586820603008779291)
XLA Ops:
  7.2 9.5 %copy.70 = bf16[1,1,128,8192]{2,1,0,3:T(2,128)(2,1)} copy(bf16[1,1,128,8192]{3,2,1,0:T(8,128)(2,1)} %bitcast.35) | data formatting | bytes 4194304 | tf_op jit(solution)/shard_map/broadcast_in_dim | solution.py:53
  17.2 45.2 %reduce.7 = bf16[8192,128]{1,0:T(8,128)(2,1)S(1)} reduce(bf16[8192,1,1,128]{3,2,1,0:T(2,128)(2,1)} %bitcast.33, bf16[]{:T(256)} %broadcast.48), dimensions={1,2}, to_apply=%bitcast.28.reduce_sub_computation | reduce | bytes 4194306
  62.4 2.0 reshape.46
  64.4 6.9 %all-to-all-start.1 = ((bf16[16,2,32768]{2,1,0:T(2,128)(2,1)}), bf16[16,2,32768]{2,1,0:T(2,128)(2,1)S(1)}, u32[]{:S(2)}, u32[]{:S(2)}) async-start(bf16[16,2,32768]{2,1,0:T(2,128)(2,1)} %reshape.46), calls=%async_computation.1 | async-start | bytes 4194304 | tf_op jit(solution)/shard_map/all_to_all | solution.py:53
  71.3 29.9 %copy.64 = bf16[1,2,64,28672]{2,1,0,3:T(2,128)(2,1)} copy(bf16[1,2,64,28672]{3,2,1,0:T(8,128)(2,1)} %param.12) | data formatting | bytes 14680064 | tf_op args[0]
  101.2 18.0 %reshape.44 = bf16[16,2,114688]{2,1,0:T(2,128)(2,1)} reshape(bf16[28672,1,2,64]{3,2,1,0:T(2,128)(2,1)} %bitcast.32) | data formatting | bytes 14680064
  119.3 5.9 %all-to-all-start = ((bf16[16,2,114688]{2,1,0:T(2,128)(2,1)}), bf16[16,2,114688]{2,1,0:T(2,128)(2,1)}, u32[]{:S(2)}, u32[]{:S(2)}) async-start(bf16[16,2,114688]{2,1,0:T(2,128)(2,1)} %reshape.44), calls=%async_computation | async-start | bytes 14680064 | tf_op jit(solution)/shard_map/all_to_all | solution.py:52
  125.7 6.7 %reshape.47 = bf16[8192,1,1,128]{3,2,1,0:T(2,128)(2,1)} reshape(bf16[16,2,32768]{2,1,0:T(2,128)(2,1)S(1)} %all-to-all-done.1) | data formatting | bytes 4194304
  132.5 8.5 %bitcast_convert_fusion = f32[1,1,128,8192]{2,1,0,3:T(1,128)} fusion(bf16[8192,1,1,128]{3,2,1,0:T(2,128)(2,1)} %reshape.47), kind=kLoop, calls=%fused_computation.33 | loop fusion | flops 1048576 | bytes 6291456 | tf_op jit(solution)/shard_map/convert_element_type | solution.py:56
  140.9 2.4 reduce_sum.19
  143.3 0.9 fusion.15
  144.3 86.1 %all-to-all-done = bf16[16,2,114688]{2,1,0:T(2,128)(2,1)} async-done(((bf16[16,2,114688]{2,1,0:T(2,128)(2,1)}), bf16[16,2,114688]{2,1,0:T(2,128)(2,1)}, u32[]{:S(2)}, u32[]{:S(2)}) %all-to-all-start) | async-done | bytes 7340064 | tf_op jit(solution)/shard_map/all_to_all | solution.py:52
  230.4 17.8 %reshape.45 = bf16[28672,1,2,64]{3,2,1,0:T(2,128)(2,1)} reshape(bf16[16,2,114688]{2,1,0:T(2,128)(2,1)} %all-to-all-done) | data formatting | bytes 14680064
  248.2 18.2 %convert_reduce_fusion = f32[2,64,1792]{1,0,2:T(2,128)S(1)} fusion(bf16[2,64,16,1792]{1,0,3,2:T(2,128)(2,1)} %bitcast.31), kind=kLoop, calls=%fused_computation | loop fusion | flops 7110656 | bytes 8257536 | tf_op jit(solution)/shard_map/reduce_sum | solution.py:55
  266.4 2.5 copy.65
  268.8 3.6 fusion.7
  272.7 91.3 %all-reduce.3.cloned.1.call-done = (f32[2,64,1792]{2,1,0:T(8,128)}, f32[128,512]{0,1:T(8,128)}) async-done(((f32[2,64,1792]{2,1,0:T(8,128)}, f32[128,512]{0,1:T(8,128)}), (f32[2,64,1792]{2,1,0:T(8,128)}, f32[128,512]{0,1:T(8,128)})) %all-reduce.3.cloned.1.call-update) | async-done | bytes 1179664 | tf_op jit(solution)/shard_map/psum | solution.py:65
  363.9 1.7 fusion.16
  365.7 2.5 fusion.17
  368.4 0.7 copy.76
  370.5 33.1 %all-gather.5.cloned.1.call-done = bf16[128,8192]{0,1:T(8,128)(2,1)} async-done(((bf16[128,512]{0,1:T(8,128)(2,1)}), bf16[128,8192]{0,1:T(8,128)(2,1)}) %all-gather.5.cloned.1.call-update) | async-done | bytes 2097168 | tf_op jit(solution)/shard_map/all_gather | solution.py:70
  403.6 4.1 copy.75
  407.7 45.3 %all-gather.3.cloned.1.call-done = bf16[2,64,28672]{2,1,0:T(8,128)(2,1)} async-done(((bf16[2,64,1792]{2,1,0:T(8,128)(2,1)}), bf16[2,64,28672]{2,1,0:T(8,128)(2,1)}) %all-gather.3.cloned.1.call-update) | async-done | bytes 7340048 | tf_op jit(solution)/shard_map/all_gather | solution.py:69
  453.0 6.8 %copy.81 = bf16[2,64,28672]{2,1,0:T(8,128)(2,1)} copy(bf16[2,64,28672]{2,1,0:T(8,128)(2,1)} %all-gather.3.cloned.1.call-done) | data formatting | bytes 14680064
  (28 shorter events, 2.9 us)
Async XLA Ops:
  64.4 54.9 %all-to-all-start.1 = ((bf16[16,2,32768]{2,1,0:T(2,128)(2,1)}), bf16[16,2,32768]{2,1,0:T(2,128)(2,1)S(1)}, u32[]{:S(2)}, u32[]{:S(2)}) async-start(bf16[16,2,32768]{2,1,0:T(2,128)(2,1)} %reshape.46), calls=%async_computation.1 | async-start | bytes 4194304 | tf_op jit(solution)/shard_map/all_to_all | solution.py:53
  119.2 5.9 %copy-start.1 = (f32[128,512]{1,0:T(8,128)S(1)}, f32[128,512]{1,0:T(8,128)}, u32[]{:S(2)}) copy-start(f32[128,512]{1,0:T(8,128)} %param.21) | copy-start | bytes 786436
  119.2 6.1 %copy-start.2 = (f32[1,128,512]{2,1,0:T(8,128)S(1)}, f32[1,128,512]{2,1,0:T(8,128)}, u32[]{:S(2)}) copy-start(f32[1,128,512]{2,1,0:T(8,128)} %param.15) | copy-start | bytes 786436
  119.2 6.2 %copy-start.3 = (f32[1,128,512]{2,1,0:T(8,128)S(1)}, f32[1,128,512]{2,1,0:T(8,128)}, u32[]{:S(2)}) copy-start(f32[1,128,512]{2,1,0:T(8,128)} %param.19) | copy-start | bytes 786436
  119.2 6.3 %copy-start.4 = (f32[1,128,512]{2,1,0:T(8,128)S(1)}, f32[1,128,512]{2,1,0:T(8,128)}, u32[]{:S(2)}) copy-start(f32[1,128,512]{2,1,0:T(8,128)} %param.17) | copy-start | bytes 786436
  119.3 111.1 %all-to-all-start = ((bf16[16,2,114688]{2,1,0:T(2,128)(2,1)}), bf16[16,2,114688]{2,1,0:T(2,128)(2,1)}, u32[]{:S(2)}, u32[]{:S(2)}) async-start(bf16[16,2,114688]{2,1,0:T(2,128)(2,1)} %reshape.44), calls=%async_computation | async-start | bytes 14680064 | tf_op jit(solution)/shard_map/all_to_all | solution.py:52
  125.1 238.8 %all-reduce.3.cloned.1.call-start = ((), (), s32[]{:S(2)}) async-start(), calls=%async_computation.4 | async-start | bytes 2359296 | tf_op jit(solution)/shard_map/psum | solution.py:65
  248.2 20.7 %copy-start = (f32[2,64,1792]{2,1,0:T(8,128)S(1)}, f32[2,64,1792]{2,1,0:T(8,128)}, u32[]{:S(2)}) copy-start(f32[2,64,1792]{2,1,0:T(8,128)} %param.20) | copy-start | bytes 2752516
  266.4 6.1 %copy-start.5 = (f32[128,512]{1,0:T(8,128)S(1)}, f32[128,512]{1,0:T(8,128)}, u32[]{:S(2)}) copy-start(f32[128,512]{1,0:T(8,128)} %param.23) | copy-start | bytes 786436
  272.5 131.2 %all-gather.5.cloned.1.call-start = ((), (), s32[]{:S(2)}) async-start(), calls=%async_computation.3 | async-start | bytes 2228224 | tf_op jit(solution)/shard_map/all_gather | solution.py:70
  365.6 87.4 %all-gather.3.cloned.1.call-start = ((), (), s32[]{:S(2)}) async-start(), calls=%async_computation.2 | async-start | bytes 7798784 | tf_op jit(solution)/shard_map/all_gather | solution.py:69
Sparse Core Ops, SparseCore 0:
  272.6 91.2 all-reduce.2
  366.2 37.4 all-gather.4
  405.9 47.0 all-gather.2
where the time goes:
time: 469 us; the launch traced here: 466 us
  waiting for transfers between devices  256 us (55%)
  local copies, waits for them, and re-layouts  101 us (22%)
  other arithmetic  82.9 us (18%)
  between operations  13.9 us (3%)
  starting transfers between devices  12.9 us (3%)
    psum x1, waiting for transfers between devices, body(): total_pair, total_down = lax.psum((drift_pair, drift_down), 'replica')  91.3 us
    unnamed x27, local copies, waits for them, and re-layouts  87.9 us
    all_to_all x1, waiting for transfers between devices, body(): lax.all_to_all(grads_pair, 'zero', split_axis=3, concat_axis=0, tiled=True)  86.1 us
    all_gather x1, waiting for transfers between devices, body(): lax.all_gather(anchor_pair_new.astype(jnp.bfloat16), 'zero', axis=2, tile...  45.3 us
    unnamed x1, other arithmetic  45.2 us
    all_gather x1, waiting for transfers between devices, body(): lax.all_gather(anchor_down_new.astype(jnp.bfloat16), 'zero', axis=1, tile...  33.1 us
    reduce_sum x1, other arithmetic, body(): summed_pair = jnp.sum(pieces_pair.astype(jnp.float32), axis=0)  18.2 us
    broadcast_in_dim x1, local copies, waits for them, and re-layouts, body(): grads_down[:, None]  9.49 us
  transfers between devices with their start and end apart: 5, of which 4 were waited for; matrix products, arithmetic and copies ran while one was open for 16% of the time, Pallas kernels for 0%

commit v1 on v0

v1 whole, which is shorter than its diff:
```python
import jax
import jax.numpy as jnp
from jax import lax
from jax.experimental import pallas as pl
from jax.experimental.pallas import tpu as pltpu
from jax.sharding import PartitionSpec as P

MESH = pl.DeviceIdType.MESH
BF = jnp.bfloat16
F32 = jnp.float32

INNER_STEP = 500
beta_one = 0.9
beta_two = 0.95
inner_rate = 0.2
decay_rate = 0.1
outer_rate = 0.7
momentum_keep = 0.9
epsilon_add = 1e-08

WIDE = {"p": 1792, "d": 512}
ROWS = 128

UNITS = [
    ("x", 0, [("p", 0, 256)]),
    ("y", 0, [("p", 1024, 256), ("d", 0, 128)]),
    ("x", 1, [("p", 256, 384)]),
    ("y", 1, [("p", 1280, 256), ("d", 128, 128)]),
    ("x", 2, [("p", 640, 384)]),
    ("y", 2, [("p", 1536, 256), ("d", 256, 256)]),
]
GATHER_LIST = [
    (0, 0, 256, "yxz"),
    (0, 256, 256, "xzy"),
    (0, 512, 128, "xyz"),
    (1, 0, 512, "yxz"),
    (1, 512, 256, "zxy"),
    (2, 0, 256, "zyx"),
    (2, 256, 384, "zyx"),
    (2, 640, 256, "xzy"),
]
GREET, MEET, CORE, LOAD, ROWS_IN, BASE, STATES, MIX, PX, FIRST, SECOND, CROSS, THIRD, BACK, FINAL, SUM, REPL, FAR, ALL, GATHER, DRAIN = range(21)
SCHEDULE = [
    (GREET,), (MEET,), (CORE, 0), (LOAD, 0), (CORE, 1), (LOAD, 2), (LOAD, 1),
    (CORE, 2), (MIX, 0), (PX, 0), (MIX, 1), (CORE, 5), (FIRST, 1), (MIX, 2),
    (LOAD, 5), (PX, 2), (BASE,), (SECOND, 1), (CORE, 3), (MIX, 5), (LOAD, 3),
    (CORE, 4), (FIRST, 5), (MIX, 3), (FIRST, 3), (THIRD, 1), (LOAD, 4), (CROSS, 0),
    (BACK, 1), (MIX, 4), (STATES, 1), (PX, 4), (FIRST, 0), (ROWS_IN,), (SECOND, 5),
    (STATES, 2), (SECOND, 3), (STATES, 3), (SUM,), (FINAL, 1), (SECOND, 0), (CROSS, 2),
    (STATES, 4), (REPL, 1), (FIRST, 2), (STATES, 0), (CROSS, 4), (THIRD, 5), (THIRD, 3),
    (STATES, 5), (FIRST, 4), (BACK, 3), (THIRD, 0), (SECOND, 2), (BACK, 5), (ALL,),
    (FAR, 1), (SECOND, 4), (GATHER, 0, 1), (REPL, 0), (GATHER, 0, 2), (FINAL, 3), (THIRD, 2),
    (THIRD, 4), (FINAL, 5), (REPL, 3), (GATHER, 1, 2), (FAR, 0), (REPL, 2), (GATHER, 0, 0),
    (GATHER, 1, 1), (REPL, 4), (FAR, 3), (GATHER, 2, 2), (REPL, 5), (FAR, 2), (GATHER, 1, 0),
    (GATHER, 0, 3), (FAR, 4), (GATHER, 0, 5), (GATHER, 2, 1), (GATHER, 0, 4), (FAR, 5), (GATHER, 0, 6),
    (GATHER, 0, 7), (GATHER, 1, 3), (GATHER, 2, 0), (GATHER, 1, 4), (GATHER, 1, 5), (GATHER, 1, 6), (GATHER, 1, 7),
    (GATHER, 2, 5), (GATHER, 3, 1), (GATHER, 4, 1), (GATHER, 2, 3), (GATHER, 3, 2), (GATHER, 4, 2), (GATHER, 3, 0),
    (GATHER, 4, 0), (GATHER, 2, 7), (GATHER, 2, 6), (GATHER, 3, 5), (GATHER, 4, 5), (GATHER, 5, 1), (GATHER, 2, 4),
    (GATHER, 6, 1), (GATHER, 3, 7), (GATHER, 4, 7), (GATHER, 3, 3), (GATHER, 4, 3), (GATHER, 3, 6), (GATHER, 4, 6),
    (GATHER, 3, 4), (GATHER, 4, 4), (GATHER, 5, 0), (GATHER, 5, 7), (GATHER, 5, 5), (GATHER, 5, 2), (GATHER, 5, 6),
    (GATHER, 5, 3), (GATHER, 6, 0), (GATHER, 5, 4), (GATHER, 6, 4), (GATHER, 6, 3), (GATHER, 6, 2), (GATHER, 6, 7),
    (GATHER, 6, 5), (GATHER, 6, 6), (DRAIN,),
]

WIDTHS = [sum(w for _, _, w in parts) for _, _, parts in UNITS]
CHUNKS = 1 + max(chunk for _, chunk, _ in UNITS)
CHUNK_WIDTHS = [sum(w for w, u in zip(WIDTHS, UNITS) if u[1] == k) for k in range(CHUNKS)]
TOTAL = sum(WIDTHS)


def unit_start(u):
    return sum(WIDTHS[v] for v in range(u) if UNITS[v][1] == UNITS[u][1])


def part_starts(u):
    at, out = 0, []
    for fam, off, w in UNITS[u][2]:
        out.append((fam, off, w, at))
        at += w
    return out


def natural(fam, off):
    return off if fam == "p" else WIDE["p"] + off


def inner_step(summed, first, second):
    first_new = beta_one * first + (1.0 - beta_one) * summed
    second_new = beta_two * second + (1.0 - beta_two) * summed * summed
    first_fix = 1.0 - beta_one**INNER_STEP
    second_fix = 1.0 - beta_two**INNER_STEP
    ratio = first_new / first_fix / (jnp.sqrt(second_new / second_fix) + epsilon_add)
    return inner_rate * ratio


class Scratch:
    def __init__(self):
        self.names, self.shapes = [], []

    def add(self, name, shape, dtype):
        self.names.append(name)
        self.shapes.append(pltpu.VMEM(shape, dtype))


def make_scratch():
    s = Scratch()
    for u, (kind, _, _) in enumerate(UNITS):
        w = WIDTHS[u]
        s.add(("own", u), (2, 4, ROWS, w), BF)
        s.add(("got", u), (2, 4, ROWS, w), BF)
        if kind == "x":
            s.add(("px", u), (4, ROWS, w), BF)
        else:
            s.add(("bx", u), (ROWS, w), BF)
        lead = () if kind == "x" else (2,)
        for name in ("t1p", "t1m", "f1p", "f1m", "f2p", "f2m"):
            s.add((name, u), lead + (ROWS // 2, w), BF)
        for name in ("first", "second"):
            s.add((name, u), (ROWS, w), F32)
        s.add(("sent", u), (2, 4, 16, w), BF)
        s.add(("repl", u), (3, 2, 16, w), BF)
        s.add(("part", u), (2, 16, w), BF)
        s.add(("far", u), (16, w), BF)
    for k in range(CHUNKS):
        s.add(("fresh", k), (16, CHUNK_WIDTHS[k]), BF)
    for name in ("anchor", "velocity", "all"):
        s.add(name, (16, TOTAL), F32)
    s.add("mine", (2, 16, TOTAL), F32)
    s.add("base", (3, 2, 16, TOTAL), F32)
    s.add("faraway", (16, TOTAL), F32)
    return s


N_SEM = 700


def step_kernel(names, *refs):
    grads = {"p": refs[0], "d": refs[1]}
    states = {
        "inner": {"p": refs[2], "d": refs[3]},
        "first": {"p": refs[4], "d": refs[5]},
        "second": {"p": refs[6], "d": refs[7]},
        "anchor": {"p": refs[8], "d": refs[9]},
        "velocity": {"p": refs[10], "d": refs[11]},
    }
    n_gather = len(GATHER_LIST)
    full = refs[12 : 12 + n_gather]
    outer = refs[12 + n_gather]
    rest = refs[13 + n_gather :]
    buf = dict(zip(names, rest))
    sems = rest[len(names)]
    count = [0]

    def sem():
        count[0] += 1
        assert count[0] <= N_SEM
        return sems.at[count[0] - 1]

    rep, zero = lax.axis_index("replica"), lax.axis_index("zero")
    xh, z = lax.div(rep, 4), lax.rem(rep, 4)
    xl, y, c = lax.div(zero, 8), lax.rem(lax.div(zero, 2), 4), lax.rem(zero, 2)
    x = xh * 2 + xl
    here = {"x": x, "y": y, "z": z}

    def place(x, y, z, c):
        return (lax.div(x, 2) * 4 + z, (lax.rem(x, 2) * 4 + y) * 2 + c)

    def near(dim, by):
        at = dict(here)
        at[dim] = lax.rem(at[dim] + by + 4, 4)
        return place(at["x"], at["y"], at["z"], c)

    sibling = place(x, y, z, 1 - c)
    pair = place(xh * 2 + 1 - xl, y, z, c)
    opposite = near("x", 2)

    def other(by):
        return lax.rem(y + by + 4, 4)

    live = {}

    def send(key, src, dst, device):
        copy = pltpu.make_async_remote_copy(
            src_ref=src, dst_ref=dst, send_sem=sem(), recv_sem=sem(), device_id=device, device_id_type=MESH
        )
        copy.start()
        live[key] = copy
        pending.append(key)

    pending, unread = [], []

    def arrive(key):
        live[key].wait_recv()
        pending.remove(key)

    local = {}

    def replica_rows(name, r, target):
        out = []
        for g in range(2):
            src = states[name]["p"].at[pl.ds(pl.multiple_of(g * 64 + r * 8, 8), 8)]
            out.append((src, target.at[pl.ds(g * 8, 8), pl.ds(0, WIDE["p"])]))
        src = states[name]["d"].at[pl.ds(pl.multiple_of(r * 16, 16), 16)]
        out.append((src, target.at[:, pl.ds(WIDE["p"], WIDE["d"])]))
        return out

    def load(u):
        mine = local["own", u] = sem()
        unread.append(("own", u))
        for fam, off, w, at in part_starts(u):

            @pl.loop(0, 8)
            def _(d, fam=fam, off=off, w=w, at=at):
                col = pl.multiple_of((d * 2 + c) * WIDE[fam] + off, 128)
                pltpu.make_async_copy(
                    grads[fam].at[:, pl.ds(col, w)],
                    buf["own", u].at[lax.div(d, 4), lax.rem(d, 4), :, pl.ds(at, w)],
                    mine,
                ).start()

    def load_states(u):
        for name in ("first", "second"):
            s = local[name, u] = sem()
            unread.append((name, u))
            for fam, off, w, at in part_starts(u):
                pltpu.make_async_copy(
                    states[name][fam].at[:, pl.ds(off, w)], buf[name, u].at[:, pl.ds(at, w)], s
                ).start()

    def load_rows():
        for name in ("anchor", "velocity"):
            s = local[name] = sem()
            unread.append(name)
            for src, dst in replica_rows(name, rep, buf[name]):
                pltpu.make_async_copy(src, dst, s).start()

    def base_send():
        for by in (1, 2, 3):
            out, into = sem(), sem()
            for b in range(2):
                for src, dst in replica_rows("inner", b * 4 + lax.rem(z + by, 4), buf["base"].at[by - 1, b]):
                    pltpu.make_async_remote_copy(
                        src_ref=src, dst_ref=dst, send_sem=out, recv_sem=into,
                        device_id=near("z", by), device_id_type=MESH,
                    ).start()
            whole = buf["base"].at[by - 1]
            live["base", by] = pltpu.make_async_remote_copy(
                src_ref=whole, dst_ref=whole, send_sem=out, recv_sem=into, device_id=near("z", by), device_id_type=MESH
            )
            pending.append(("base", by))
        s = local["mine"] = sem()
        unread.append("mine")
        for b in range(2):
            for src, dst in replica_rows("inner", b * 4 + z, buf["mine"].at[b]):
                pltpu.make_async_copy(src, dst, s).start()

    def base_sum():
        loaded("mine")
        for by in (1, 2, 3):
            arrive(("base", by))
        mine, got = buf["mine"], buf["base"]

        @pl.loop(0, TOTAL // 256)
        def _(i):
            cols = pl.ds(pl.multiple_of(i * 256, 256), 256)
            for b in range(2):
                mine[b, :, cols] = mine[b, :, cols] + got[0, b, :, cols] + got[1, b, :, cols] + got[2, b, :, cols]

        send("faraway", mine.at[1 - xh], buf["faraway"], opposite)

    def base_all():
        arrive("faraway")
        loaded("anchor")
        loaded("velocity")

        @pl.loop(0, TOTAL // 256)
        def _(i):
            cols = pl.ds(pl.multiple_of(i * 256, 256), 256)
            kept = (1.0 - inner_rate * decay_rate) / 8.0
            buf["all"][:, cols] = kept * (buf["mine"][xh, :, cols] + buf["faraway"][:, cols])

    def loaded(key):
        pltpu.make_async_copy(buf[key], buf[key], local[key]).wait()
        unread.remove(key)

    friends = [sibling] + [near(dim, by) for dim in "xyz" for by in (1, 2, 3)]
    gate = pltpu.get_barrier_semaphore()

    def greet():
        for friend in friends:
            pl.semaphore_signal(gate, inc=1, device_id=friend, device_id_type=MESH)

    def meet():
        pl.semaphore_wait(gate, len(friends))

    def core(u):
        out, into = sem(), sem()
        for fam, off, w, at in part_starts(u):

            @pl.loop(0, 8)
            def _(d, fam=fam, off=off, w=w, at=at):
                col = pl.multiple_of((d * 2 + 1 - c) * WIDE[fam] + off, 128)
                pltpu.make_async_remote_copy(
                    src_ref=grads[fam].at[:, pl.ds(col, w)],
                    dst_ref=buf["got", u].at[lax.div(d, 4), lax.rem(d, 4), :, pl.ds(at, w)],
                    send_sem=out,
                    recv_sem=into,
                    device_id=sibling,
                    device_id_type=MESH,
                ).start()
        live["core", u] = pltpu.make_async_remote_copy(
            src_ref=buf["got", u],
            dst_ref=buf["got", u],
            send_sem=out,
            recv_sem=into,
            device_id=sibling,
            device_id_type=MESH,
        )
        pending.append(("core", u))

    def add_rows(dst, src, rows):
        @pl.loop(0, rows // 32)
        def _(i):
            at = pl.ds(pl.multiple_of(i * 32, 32), 32)
            dst[at, :] = dst[at, :] + src[at, :]

    def add_blocks(own, got, xl_at):
        @pl.loop(0, 4 * ROWS // 32)
        def _(i):
            b, at = lax.div(i, 4), pl.ds(pl.multiple_of(lax.rem(i, 4) * 32, 32), 32)
            own[xl_at, b, at, :] = own[xl_at, b, at, :] + got[xl_at, b, at, :]

    def mix(u):
        loaded(("own", u))
        arrive(("core", u))
        own, got = buf["own", u], buf["got", u]
        add_blocks(own, got, 1 - xl)
        add_blocks(own, got, xl)

    def send_pair(u):
        send(("px", u), buf["own", u].at[1 - xl], buf["px", u], pair)

    def cross(u):
        arrive(("px", u))
        own, px = buf["own", u], buf["px", u]

        @pl.loop(0, 4 * ROWS // 32)
        def _(i):
            b, at = lax.div(i, 4), pl.ds(pl.multiple_of(lax.rem(i, 4) * 32, 32), 32)
            own[xl, b, at, :] = own[xl, b, at, :] + px[b, at, :]

    half = ROWS // 2
    low, high = pl.ds(0, half), pl.ds(half, half)

    def block(u, at, rows):
        own = buf["own", u]
        return own.at[xl, at, rows] if UNITS[u][0] == "x" else own.at[:, at, rows]

    def first(u):
        send(("t1p", u), block(u, other(2), low), buf["t1p", u], near("y", 1))
        send(("t1m", u), block(u, other(2), high), buf["t1m", u], near("y", -1))
        send(("f1p", u), block(u, other(1), high), buf["f1p", u], near("y", 1))
        send(("f1m", u), block(u, other(-1), low), buf["f1m", u], near("y", -1))

    def add_into(u, at, start, src):
        own = buf["own", u]
        if UNITS[u][0] == "x":
            add_rows(own.at[xl, at, pl.ds(start, half)], src, half)
        else:
            for i in range(2):
                add_rows(own.at[i, at, pl.ds(start, half)], src.at[i], half)

    def second(u):
        arrive(("t1p", u))
        add_into(u, other(1), 0, buf["t1p", u])
        send(("f2p", u), block(u, other(1), low), buf["f2p", u], near("y", 1))
        arrive(("t1m", u))
        add_into(u, other(-1), half, buf["t1m", u])
        send(("f2m", u), block(u, other(-1), high), buf["f2m", u], near("y", -1))

    def update(u, h, t, summed):
        at = pl.ds(pl.multiple_of(h * half + t * 16, 16), 16)
        new = inner_step(summed, buf["first", u][at, :], buf["second", u][at, :])
        sent = buf["sent", u]
        for fam, _, w, start in part_starts(u):
            cols = pl.ds(start, w)
            piece = new[:, start : start + w]
            if fam == "p":
                sent[lax.div(t, 2), 2 * lax.rem(t, 2), h * 8 : h * 8 + 8, cols] = piece[:8].astype(BF)
                sent[lax.div(t, 2), 2 * lax.rem(t, 2) + 1, h * 8 : h * 8 + 8, cols] = piece[8:].astype(BF)
            else:
                sent[h, t, :, cols] = piece.astype(BF)

    def states_ready(u):
        for name in ("first", "second"):
            loaded((name, u))

    def third(u):
        for name in ("f1p", "f1m", "f2p", "f2m"):
            arrive((name, u))
        own = buf["own", u]
        if UNITS[u][0] == "x":
            states_ready(u)
        for h, (one, two) in enumerate((("f2p", "f1m"), ("f1p", "f2m"))):
            if UNITS[u][0] == "x":

                @pl.loop(0, 4)
                def _(t, h=h, one=one, two=two):
                    at = pl.ds(pl.multiple_of(t * 16, 16), 16)
                    mine = own[xl, y, pl.ds(pl.multiple_of(h * half + t * 16, 16), 16), :].astype(F32)
                    total = mine + buf[one, u][at, :].astype(F32) + buf[two, u][at, :].astype(F32)
                    update(u, h, t, total)
            else:

                @pl.loop(0, 8)
                def _(i, h=h, one=one, two=two):
                    b, t = lax.div(i, 4), lax.rem(i, 4)
                    at = pl.ds(pl.multiple_of(t * 16, 16), 16)
                    to = pl.ds(pl.multiple_of(h * half + t * 16, 16), 16)
                    total = own[b, y, to, :].astype(F32) + buf[one, u][b, at, :].astype(F32)
                    own[b, y, to, :] = (total + buf[two, u][b, at, :].astype(F32)).astype(BF)
        if UNITS[u][0] == "x":
            spread(u)

    def back(u):
        send(("bx", u), buf["own", u].at[1 - xl, y], buf["bx", u], pair)

    def final(u):
        arrive(("bx", u))
        states_ready(u)
        own, bx = buf["own", u], buf["bx", u]
        for h in range(2):

            @pl.loop(0, 4)
            def _(t, h=h):
                at = pl.ds(pl.multiple_of(h * half + t * 16, 16), 16)
                update(u, h, t, own[xl, y, at, :].astype(F32) + bx[at, :].astype(F32))

        spread(u)

    def spread(u):
        for by in (1, 2, 3):
            send(("repl", u, by), buf["sent", u].at[:, lax.rem(z + by, 4)], buf["repl", u].at[by - 1], near("z", by))

    def repl(u):
        for by in (1, 2, 3):
            arrive(("repl", u, by))
        sent, got, part = buf["sent", u], buf["repl", u], buf["part", u]
        for b in (1 - xh, xh):
            total = sent[b, z].astype(F32) + got[0, b].astype(F32) + got[1, b].astype(F32) + got[2, b].astype(F32)
            part[b] = total.astype(BF)
        send(("far", u), part.at[1 - xh], buf["far", u], opposite)

    def far(u):
        arrive(("far", u))
        for fam, off, w, at in part_starts(u):
            cols, to = pl.ds(at, w), pl.ds(natural(fam, off), w)
            steps = buf["part", u][xh, :, cols].astype(F32) + buf["far", u][:, cols].astype(F32)
            anchor = buf["anchor"][:, to]
            pseudo = anchor - (buf["all"][:, to] - steps / 8.0)
            velocity_next = momentum_keep * buf["velocity"][:, to] + pseudo
            anchor_next = anchor - outer_rate * (pseudo + momentum_keep * velocity_next)
            outer[0, :, to] = anchor_next
            outer[1, :, to] = velocity_next
            buf["fresh", UNITS[u][1]][:, pl.ds(unit_start(u) + at, w)] = anchor_next.astype(BF)

    def slot(dim, by=0):
        at = lax.rem(here[dim] + by + 4, 4)
        return lax.rem(at, 2) * 2 + lax.div(at, 2) if dim == "x" else at

    def gather(stage, g):
        k, at, w, (d1, d2, d3) = GATHER_LIST[g]
        whole = full[g]
        if stage == 0:
            mine = whole.at[c, slot(d3), slot(d2), slot(d1)]
            mine[...] = buf["fresh", k][:, pl.ds(at, w)]
            for by in (1, 3, 2):
                send(("g", g, "0", by), mine, mine, near(d1, by))
        elif stage == 1:
            for by in (1, 3, 2):
                arrive(("g", g, "0", by))
            mine = whole.at[c, slot(d3), slot(d2)]
            for by in (1, 3, 2):
                send(("g", g, "1", by), mine, mine, near(d2, by))
        elif stage == 2:
            for by in (1, 3, 2):
                arrive(("g", g, "1", by))
            for turn in (0, 1):
                for by, part in ((1, 0), (3, 2)):
                    some = whole.at[c, slot(d3), pl.ds(part if turn == 0 else 2 - part, 2)]
                    send(("g", g, "2", by, turn), some, some, near(d3, by))
            mine = whole.at[c, slot(d3)]
            send(("g", g, "s", 0), mine, mine, sibling)
        elif stage == 3:
            for by, part in ((1, 0), (3, 2)):
                arrive(("g", g, "2", by, 0))
                some = whole.at[c, slot(d3, -by), pl.ds(part, 2)]
                send(("g", g, "3", by), some, some, near(d3, by))
        elif stage == 4:
            for by in (1, 3):
                arrive(("g", g, "2", by, 1))
                got = whole.at[c, slot(d3, -by)]
                send(("g", g, "s", by), got, got, sibling)
        elif stage == 5:
            for by, part in ((1, 0), (3, 2)):
                arrive(("g", g, "3", by))
                some = whole.at[c, slot(d3, 2), pl.ds(part, 2)]
                send(("g", g, "t", by), some, some, sibling)
        else:
            for key in (("s", 0), ("s", 1), ("s", 3), ("t", 1), ("t", 3)):
                arrive(("g", g) + key)

    def drain():
        for key in list(pending):
            arrive(key)
        for key in list(unread):
            loaded(key)
        for copy in live.values():
            copy.wait_send()

    acts = {
        GREET: greet, MEET: meet, CORE: core, LOAD: load, ROWS_IN: load_rows, BASE: base_send, STATES: load_states,
        MIX: mix, PX: send_pair, FIRST: first, SECOND: second, CROSS: cross, THIRD: third, BACK: back, FINAL: final,
        SUM: base_sum, REPL: repl, FAR: far, ALL: base_all, GATHER: gather, DRAIN: drain,
    }
    for act, *where in SCHEDULE:
        acts[act](*where)


def gather_shape(g):
    _, _, w, _ = GATHER_LIST[g]
    return (2, 4, 4, 4, 16, w)


def run_step(args):
    s = make_scratch()
    outs = [pltpu.VMEM(gather_shape(g), BF) for g in range(len(GATHER_LIST))]
    outs.append(pltpu.VMEM((2, 16, TOTAL), F32))

    def kernel(*refs):
        step_kernel(s.names, *refs)

    return pl.pallas_call(
        kernel,
        out_shape=outs,
        in_specs=[pl.BlockSpec(memory_space=pltpu.HBM)] * 12,
        out_specs=[pl.BlockSpec(memory_space=pltpu.VMEM)] * len(outs),
        scratch_shapes=s.shapes + [pltpu.SemaphoreType.DMA((N_SEM,))],
        compiler_params=pltpu.CompilerParams(
            collective_id=0, has_side_effects=True, vmem_limit_bytes=48 * 2**20
        ),
        name="outer_step",
    )(*args)


def column_pieces():
    out = []
    for g, (k, at, w, _) in enumerate(GATHER_LIST):
        for u in range(len(UNITS)):
            if UNITS[u][1] != k:
                continue
            for fam, off, wide, start in part_starts(u):
                begin = unit_start(u) + start
                lo, hi = max(begin, at), min(begin + wide, at + w)
                if lo < hi:
                    out.append((g, lo - at, hi - lo, fam, off + lo - begin))
    return out


def place_kernel(*refs):
    n = len(GATHER_LIST)
    full, outer = refs[:n], refs[n]
    weights_pair, weights_down, anchor_pair, anchor_down, velocity_pair, velocity_down = refs[n + 1 : n + 7]
    pair_rows, down_rows, sems = refs[n + 7 :]

    for i, (pair, down) in enumerate(((anchor_pair, anchor_down), (velocity_pair, velocity_down))):
        pair[0] = outer[i, :8, : WIDE["p"]]
        pair[1] = outer[i, 8:, : WIDE["p"]]
        down[...] = outer[i, :, WIDE["p"] :]

    @pl.loop(0, 16)
    def _(q):
        c, y, xl = lax.rem(q, 2), lax.rem(lax.div(q, 2), 4), lax.div(q, 8)

        def block(g, r):
            index = {"x": xl * 2 + r // 4, "y": y, "z": r % 4}
            return (c,) + tuple(index[d] for d in reversed(GATHER_LIST[g][3]))

        start = {fam: pl.multiple_of(q * WIDE[fam], 128) for fam in WIDE}
        for g, at, w, fam, col in column_pieces():
            to = pl.ds(pl.multiple_of(start[fam] + col, 128), w)
            for m in range(4):
                one = full[g][block(g, 2 * m) + (slice(None), slice(at, at + w))]
                two = full[g][block(g, 2 * m + 1) + (slice(None), slice(at, at + w))]
                if fam == "d":
                    down_rows[32 * m : 32 * m + 16, to] = one
                    down_rows[32 * m + 16 : 32 * m + 32, to] = two
                else:
                    for half in range(2):
                        rows = slice(8 * half, 8 * half + 8)
                        pair_rows[half, 16 * m : 16 * m + 16, to] = jnp.concatenate([one[rows], two[rows]], axis=0)
        cols = pl.ds(start["p"], WIDE["p"])
        pltpu.make_async_copy(pair_rows.at[:, :, cols], weights_pair.at[:, :, cols], sems.at[0]).start()
        cols = pl.ds(start["d"], WIDE["d"])
        pltpu.make_async_copy(down_rows.at[:, cols], weights_down.at[:, cols], sems.at[1]).start()

    pltpu.make_async_copy(pair_rows, weights_pair, sems.at[0]).wait()
    pltpu.make_async_copy(down_rows, weights_down, sems.at[1]).wait()


def run_place(full, outer):
    vmem = pl.BlockSpec(memory_space=pltpu.VMEM)
    hbm = pl.BlockSpec(memory_space=pltpu.HBM)
    return pl.pallas_call(
        place_kernel,
        out_shape=[
            jax.ShapeDtypeStruct((2, 64, 28672), BF),
            jax.ShapeDtypeStruct((128, 8192), BF),
            jax.ShapeDtypeStruct((2, 8, 1792), F32),
            jax.ShapeDtypeStruct((16, 512), F32),
            jax.ShapeDtypeStruct((2, 8, 1792), F32),
            jax.ShapeDtypeStruct((16, 512), F32),
        ],
        in_specs=[vmem] * (len(full) + 1),
        out_specs=[hbm, hbm, vmem, vmem, vmem, vmem],
        scratch_shapes=[
            pltpu.VMEM((2, 64, 28672), BF),
            pltpu.VMEM((128, 8192), BF),
            pltpu.SemaphoreType.DMA((2,)),
        ],
        compiler_params=pltpu.CompilerParams(vmem_limit_bytes=32 * 2**20),
        name="place",
    )(*full, outer)


def body(
    grads_pair,
    grads_down,
    inner_pair,
    inner_down,
    first_pair,
    first_down,
    second_pair,
    second_down,
    anchor_pair,
    anchor_down,
    velocity_pair,
    velocity_down,
):
    args = [
        grads_pair.reshape(128, 28672),
        grads_down.reshape(128, 8192),
        inner_pair.reshape(128, 1792),
        inner_down.reshape(128, 512),
        first_pair.reshape(128, 1792),
        first_down.reshape(128, 512),
        second_pair.reshape(128, 1792),
        second_down.reshape(128, 512),
        anchor_pair.reshape(128, 1792),
        anchor_down,
        velocity_pair.reshape(128, 1792),
        velocity_down,
    ]
    *full, outer = run_step(args)
    return tuple(run_place(full, outer))


def solution(mesh):
    in_specs = (
        P(("replica", "zero"), None, None, None),
        P(("replica", "zero"), None, None),
        P("replica", None, None, "zero"),
        P("replica", None, "zero"),
        P("replica", None, None, "zero"),
        P("replica", None, "zero"),
        P("replica", None, None, "zero"),
        P("replica", None, "zero"),
        P(None, None, "zero"),
        P(None, "zero"),
        P(None, None, "zero"),
        P(None, "zero"),
    )
    out_specs = (
        P(),
        P(),
        P(None, "replica", "zero"),
        P("replica", "zero"),
        P(None, "replica", "zero"),
        P("replica", "zero"),
    )
    return jax.shard_map(body, mesh=mesh, in_specs=in_specs, out_specs=out_specs, check_vma=False)
```

time: 469 us -> 87.2 us (0.19)
  waiting for transfers between devices: 256 us -> 0 us
  local copies, waits for them, and re-layouts: 101 us -> 0 us
  Pallas kernels: 0 us -> 86.3 us
  other arithmetic: 82.9 us -> 0 us
  between operations: 13.9 us -> 0.64 us
  starting transfers between devices: 12.9 us -> 0 us
    psum x1 -> x0, waiting for transfers between devices: 91.3 us -> none  [body(): total_pair, total_down = lax.psum((drift_pair, drift_down), 'replica')]
    unnamed x27 -> x0, local copies, waits for them, and re-layouts: 87.9 us -> none
    pallas_call x0 -> x2, Pallas kernels: none -> 86.3 us  [the longest x1 81.9 us: run_step(): pl.pallas_call(kernel, out_shape=outs, in_specs=[pl.BlockSpec(memory_spac...]
    all_to_all x2 -> x0, waiting for transfers between devices: 86.1 us -> none  [the longest x1 86.1 us: body(): lax.all_to_all(grads_pair, 'zero', split_axis=3, concat_axis=0, tiled=True)]
    all_gather x2 -> x0, waiting for transfers between devices: 78.4 us -> none  [the longest x1 45.3 us: body(): lax.all_gather(anchor_pair_new.astype(jnp.bfloat16), 'zero', axis=2, tile...]
    unnamed x1 -> x0, other arithmetic: 45.2 us -> none
    reduce_sum x2 -> x0, other arithmetic: 20.6 us -> none  [the longest x1 18.2 us: body(): summed_pair = jnp.sum(pieces_pair.astype(jnp.float32), axis=0)]
    all_to_all x2 -> x0, starting transfers between devices: 12.8 us -> none  [the longest x1 6.91 us: body(): lax.all_to_all(grads_down[:, None], 'zero', split_axis=3, concat_axis=0,...]
  transfers between devices with their start and end apart: 5 -> 0, of which waited for: 4 -> 0; matrix products, arithmetic and copies ran while one was open for 16% -> 0% of each run, Pallas kernels for 0% -> 0%
where the time goes in v1:
time: 87.2 us; the launch traced here: 86.9 us
  Pallas kernels  86.3 us (99%)
    pallas_call x1, Pallas kernels, run_step(): pl.pallas_call(kernel, out_shape=outs, in_specs=[pl.BlockSpec(memory_spac...  81.9 us
    pallas_call x1, Pallas kernels, run_place(): pl.pallas_call(place_kernel, out_shape=[jax.ShapeDtypeStruct((2, 64, 2867...  4.43 us

profile of v1, /device:TPU:1, one launch (start us, length us, event | category | flops | bytes accessed | tf_op | source)
XLA Modules:
  0.0 86.9 jit_solution(13680341835851798795)
XLA Ops:
  0.6 81.9 %outer_step.1 = (bf16[2,4,4,4,16,256]{5,4,3,2,1,0:T(8,128)(2,1)S(1)}, bf16[2,4,4,4,16,256]{5,4,3,2,1,0:T(8,128)(2,1)S(1)}, bf16[2,4,4,4,16,128]{5,4,3,2,1,0:T(8,...) custom-call(bf16[128,28672]{1,0:T(8,128)(2,1)} %bitcast.10, ...), custom_call_target="tpu_custom_call" | custom-call | tf_op jit(solution)/shard_map/outer_step/pallas_call | solution.py:543
  82.5 4.4 %place.1 = (bf16[2,64,28672]{2,1,0:T(8,128)(2,1)}, bf16[128,8192]{1,0:T(8,128)(2,1)}, f32[2,8,1792]{2,1,0:T(8,128)}, f32[16,512]{1,0:T(8,128)}, f32[2,8,1792]{2,1,0:T(8,128)}, /*index=5*/f32[16,512]{1,0:T(8,128)}) custom-call(bf16[2,4,4,4,16,256]{5,4,3,2,1,0:T(8,128)(2,1)S(1)} %get-tuple-element.15.refs_0_, ...), custom_call_target="tpu_custom_call" | custom-call | tf_op jit(solution)/shard_map/place/pallas_call | solution.py:614

commit v2 on v1

--- a/solution.py
+++ b/solution.py
@@ -43,7 +43,7 @@
 SCHEDULE = [
     (GREET,), (MEET,), (CORE, 0), (LOAD, 0), (CORE, 1), (LOAD, 2), (LOAD, 1),
     (CORE, 2), (MIX, 0), (PX, 0), (MIX, 1), (CORE, 5), (FIRST, 1), (MIX, 2),
-    (LOAD, 5), (PX, 2), (BASE,), (SECOND, 1), (CORE, 3), (MIX, 5), (LOAD, 3),
+    (BASE,), (LOAD, 5), (PX, 2), (SECOND, 1), (CORE, 3), (MIX, 5), (LOAD, 3),
     (CORE, 4), (FIRST, 5), (MIX, 3), (FIRST, 3), (THIRD, 1), (LOAD, 4), (CROSS, 0),
     (BACK, 1), (MIX, 4), (STATES, 1), (PX, 4), (FIRST, 0), (ROWS_IN,), (SECOND, 5),
     (STATES, 2), (SECOND, 3), (STATES, 3), (SUM,), (FINAL, 1), (SECOND, 0), (CROSS, 2),
@@ -57,7 +57,7 @@
     (GATHER, 2, 5), (GATHER, 3, 1), (GATHER, 4, 1), (GATHER, 2, 3), (GATHER, 3, 2), (GATHER, 4, 2), (GATHER, 3, 0),
     (GATHER, 4, 0), (GATHER, 2, 7), (GATHER, 2, 6), (GATHER, 3, 5), (GATHER, 4, 5), (GATHER, 5, 1), (GATHER, 2, 4),
     (GATHER, 6, 1), (GATHER, 3, 7), (GATHER, 4, 7), (GATHER, 3, 3), (GATHER, 4, 3), (GATHER, 3, 6), (GATHER, 4, 6),
-    (GATHER, 3, 4), (GATHER, 4, 4), (GATHER, 5, 0), (GATHER, 5, 7), (GATHER, 5, 5), (GATHER, 5, 2), (GATHER, 5, 6),
+    (GATHER, 3, 4), (GATHER, 4, 4), (GATHER, 5, 0), (GATHER, 5, 7), (GATHER, 5, 2), (GATHER, 5, 5), (GATHER, 5, 6),
     (GATHER, 5, 3), (GATHER, 6, 0), (GATHER, 5, 4), (GATHER, 6, 4), (GATHER, 6, 3), (GATHER, 6, 2), (GATHER, 6, 7),
     (GATHER, 6, 5), (GATHER, 6, 6), (DRAIN,),
 ]
@@ -474,13 +474,13 @@
         if stage == 0:
             mine = whole.at[c, slot(d3), slot(d2), slot(d1)]
             mine[...] = buf["fresh", k][:, pl.ds(at, w)]
-            for by in (1, 3, 2):
+            for by in (2, 1, 3):
                 send(("g", g, "0", by), mine, mine, near(d1, by))
         elif stage == 1:
             for by in (1, 3, 2):
                 arrive(("g", g, "0", by))
             mine = whole.at[c, slot(d3), slot(d2)]
-            for by in (1, 3, 2):
+            for by in (2, 1, 3):
                 send(("g", g, "1", by), mine, mine, near(d2, by))
         elif stage == 2:
             for by in (1, 3, 2):
@@ -489,14 +489,14 @@
                 for by, part in ((1, 0), (3, 2)):
                     some = whole.at[c, slot(d3), pl.ds(part if turn == 0 else 2 - part, 2)]
                     send(("g", g, "2", by, turn), some, some, near(d3, by))
-            mine = whole.at[c, slot(d3)]
-            send(("g", g, "s", 0), mine, mine, sibling)
         elif stage == 3:
             for by, part in ((1, 0), (3, 2)):
                 arrive(("g", g, "2", by, 0))
                 some = whole.at[c, slot(d3, -by), pl.ds(part, 2)]
                 send(("g", g, "3", by), some, some, near(d3, by))
         elif stage == 4:
+            mine = whole.at[c, slot(d3)]
+            send(("g", g, "s", 0), mine, mine, sibling)
             for by in (1, 3):
                 arrive(("g", g, "2", by, 1))
                 got = whole.at[c, slot(d3, -by)]

time: 87.2 us -> 86.9 us (level)
  no operation moved by 1% of the time
where the time goes in v2:
time: 86.9 us; the launch traced here: 86.7 us
  Pallas kernels  86 us (99%)
    pallas_call x1, Pallas kernels, run_step(): pl.pallas_call(kernel, out_shape=outs, in_specs=[pl.BlockSpec(memory_spac...  81.6 us
    pallas_call x1, Pallas kernels, run_place(): pl.pallas_call(place_kernel, out_shape=[jax.ShapeDtypeStruct((2, 64, 2867...  4.43 us

profile of v2, /device:TPU:1, one launch (start us, length us, event | category | flops | bytes accessed | tf_op | source)
XLA Modules:
  0.0 86.7 jit_solution(1723475116215686344)
XLA Ops:
  0.6 81.6 %outer_step.1 = (bf16[2,4,4,4,16,256]{5,4,3,2,1,0:T(8,128)(2,1)S(1)}, bf16[2,4,4,4,16,256]{5,4,3,2,1,0:T(8,128)(2,1)S(1)}, bf16[2,4,4,4,16,128]{5,4,3,2,1,0:T(8,...) custom-call(bf16[128,28672]{1,0:T(8,128)(2,1)} %bitcast.10, ...), custom_call_target="tpu_custom_call" | custom-call | tf_op jit(solution)/shard_map/outer_step/pallas_call | solution.py:543
  82.2 4.4 %place.1 = (bf16[2,64,28672]{2,1,0:T(8,128)(2,1)}, bf16[128,8192]{1,0:T(8,128)(2,1)}, f32[2,8,1792]{2,1,0:T(8,128)}, f32[16,512]{1,0:T(8,128)}, f32[2,8,1792]{2,1,0:T(8,128)}, /*index=5*/f32[16,512]{1,0:T(8,128)}) custom-call(bf16[2,4,4,4,16,256]{5,4,3,2,1,0:T(8,128)(2,1)S(1)} %get-tuple-element.15.refs_0_, ...), custom_call_target="tpu_custom_call" | custom-call | tf_op jit(solution)/shard_map/place/pallas_call | solution.py:614
